TPU v7x, 128 devices: a whole 4x4x4 slice. The times are simulated.
128 devices in a mesh: outer: 4 (over x_lo, core), vocab: 32 (over y, z, x_hi).
Axes of the slice: x: 4 (x_hi: 2, x_lo: 2; x = x_hi * 2 + x_lo), y: 4, z: 4, core: 2. Of those that a mesh axis runs over, the one named last changes fastest.
Arguments:
- hidden: bfloat16 [2048, 4096], P(('outer', 'vocab')), parts along dimension 0, may hold values from -96 to 96
- targets: int32 [2048], P(('outer', 'vocab')), parts along dimension 0, may hold values from 0 to 65535
- head: bfloat16 [16384, 65536], P('outer', 'vocab'), parts along dimension 0, may hold values from -1 to 1
- global_frag: float32 [128, 65536], P(None, 'vocab'), may hold values from -6 to 6
- momentum: float32 [128, 65536], P(None, 'vocab'), may hold values from -6 to 6
- peer_delta: float32 [512, 65536], P('outer', 'vocab'), parts along dimension 0, may hold values from -6 to 6
Outputs:
- loss: float32 [4], P('outer'), parts along dimension 0
- hidden_grad: bfloat16 [2048, 4096], P(('outer', 'vocab')), parts along dimension 0
- new_global: float32 [512, 65536], P('outer', 'vocab'), parts along dimension 0
- new_momentum: float32 [512, 65536], P('outer', 'vocab'), parts along dimension 0
There are 4 independent parts, one for each index of `outer`. A program takes and returns all parts, laid end to end along the dimension named above; an argument that names none is the same for every part. Nothing has to cross between parts.
All inputs are finite; a program needn't handle non-finite values.
Results may differ from a plain program's by a relative error of at most 0.0031.
Values may be sent and summed in bfloat16 or wider, within the bound.
A program may use at most 128 MiB of HBM per device.

v0:
```python
import jax
import jax.numpy as jnp
from jax import lax
from jax.sharding import PartitionSpec as P

FRAG = 128
REPLICAS = 4


def body(hidden, targets, head, global_frag, momentum, peer_delta):
    rows_all, ids_all = (
        lax.all_gather(hidden, "vocab", axis=0, tiled=True),
        lax.all_gather(targets, "vocab", axis=0, tiled=True),
    )
    row_count = rows_all.shape[0]
    width = head.shape[1]
    logits = jnp.dot(rows_all, head, preferred_element_type=jnp.float32)
    offset = lax.axis_index("vocab") * width
    columns = offset + jnp.arange(width, dtype=jnp.int32)
    onehot = (columns[None, :] == ids_all[:, None]).astype(jnp.float32)
    local_max = jnp.max(logits, axis=1)
    local_pick = jnp.sum(logits * onehot, axis=1)
    top = lax.pmax(local_max, "vocab")
    total, picked = lax.psum((jnp.sum(jnp.exp(logits - top[:, None]), axis=1), local_pick), "vocab")
    loss = jnp.mean(top + jnp.log(total) - picked).reshape((1,))
    dlogits = ((jnp.exp(logits - top[:, None]) / total[:, None] - onehot) / row_count).astype(
        jnp.bfloat16
    )
    own_rows = hidden.shape[0]
    partial_grad = lax.dot_general(
        dlogits, head, (((1,), (1,)), ((), ())), preferred_element_type=jnp.float32
    )
    summed = lax.psum(partial_grad, "vocab")
    hidden_grad = lax.dynamic_slice_in_dim(
        summed, lax.axis_index("vocab") * own_rows, own_rows, 0
    ).astype(jnp.bfloat16)
    frag_grad = lax.dot_general(
        rows_all[:, :FRAG], dlogits, (((0,), (0,)), ((), ())), preferred_element_type=jnp.float32
    )
    local_frag = head[:FRAG].astype(jnp.float32) - 1.0 * frag_grad
    pseudo = (global_frag - local_frag + peer_delta) / REPLICAS
    new_momentum = 0.9 * momentum + pseudo
    new_global = global_frag - 0.7 * (pseudo + 0.9 * new_momentum)
    return (loss, hidden_grad, new_global, new_momentum)


def solution(mesh):
    in_specs = (
        P(("outer", "vocab"), None),
        P(("outer", "vocab")),
        P("outer", "vocab"),
        P(None, "vocab"),
        P(None, "vocab"),
        P("outer", "vocab"),
    )
    out_specs = (P("outer"), P(("outer", "vocab"), None), P("outer", "vocab"), P("outer", "vocab"))
    return jax.shard_map(body, mesh=mesh, in_specs=in_specs, out_specs=out_specs, check_vma=False)
```

profile of v0, /device:TPU:6, one launch (start us, length us, event | category | flops | bytes accessed | tf_op | source)
XLA Modules:
  0.0 685.4 jit_solution(5436039864729366553)
XLA Ops:
  7.2 0.0 copy-start.1
  7.2 0.0 copy-start.2
  7.2 0.0 all-gather.2.cloned.1.call-start
  7.2 0.7 all-gather.2.cloned.1.call-update
  7.9 0.0 copy-start.7
  7.9 0.0 copy-start.6
  8.0 1.1 slice.6
  9.0 0.3 copy.17
  9.3 2.5 copy.14
  11.9 0.0 copy-done.1
  11.9 1.3 copy.13
  13.2 0.0 copy-done.2
  13.2 1.3 copy.12
  14.5 0.0 copy-done.7
  14.5 0.6 dynamic-slice
  15.7 0.0 copy-done.6
  15.8 0.2 dynamic-update-slice
  16.0 22.2 %all-reduce = s32[512]{0:T(512)S(1)} all-reduce(s32[512]{0:T(512)S(1)} %dynamic-update-slice), channel_id=1, replica_groups=mesh['outer'=4,'vocab'=32] {'vocab'}, use_global_device_ids=true, to_apply=%add | all-reduce | flops 512 | bytes 4096
  38.2 54.3 %all-gather.2.cloned.1.call-done = bf16[512,4096]{1,0:T(8,128)(2,1)} async-done(((bf16[16,4096]{1,0:T(8,128)(2,1)}), bf16[512,4096]{1,0:T(8,128)(2,1)}) %all-gather.2.cloned.1.call-update) | async-done | bytes 4194320 | tf_op jit(solution)/shard_map/all_gather | solution.py:12
  92.4 15.0 %fusion.13 = (f32[512]{0:T(512)S(1)}, f32[512,2048]{1,0:T(8,128)}) fusion(bf16[512,4096]{1,0:T(8,128)(2,1)} %all-gather.2.cloned.1.call-done, bf16[4096,2048]{1,0:T(8,128)(2,1)} %param.8), kind=kOutput, calls=%fused_computation.20 | convolution fusion | flops 8590983168 | bytes 25167872 | tf_op jit(solution)/shard_map/dot_general | solution.py:17
  107.4 91.2 %pmax.7 = f32[512]{0:T(512)S(1)} all-reduce(f32[512]{0:T(512)S(1)} %get-tuple-element.14), channel_id=1, replica_groups=mesh['outer'=4,'vocab'=32] {'vocab'}, use_global_device_ids=true, to_apply=%region_1.0 | all-reduce | flops 512 | bytes 4096 | tf_op jit(solution)/shard_map/pmax | solution.py:23
  198.6 3.3 fusion.4
  201.9 95.0 %psum.21 = f32[512]{0:T(512)S(1)} all-reduce(f32[512]{0:T(512)S(1)} %get-tuple-element.8), channel_id=1, replica_groups=mesh['outer'=4,'vocab'=32] {'vocab'}, use_global_device_ids=true, to_apply=%region_3.0 | all-reduce | flops 512 | bytes 4096 | tf_op jit(solution)/shard_map/psum | solution.py:24
  297.0 0.0 copy-start
  297.0 0.0 copy-start.3
  297.0 0.0 copy-start.4
  297.0 0.0 copy-start.5
  297.0 18.2 %fusion.11 = f32[512,4096]{1,0:T(8,128)} fusion(bf16[4096,2048]{1,0:T(8,128)(2,1)} %param.8, f32[512,2048]{1,0:T(8,128)} %get-tuple-element.15, f32[512]{0:T(512)S(1)} %psum.21, s32[2048]{0:T(1024)S(1)} %iota_add_fusion, f32[512]{0:T(512)S(1)} %pmax.7, s32[512]{0:T(512)S(1)} %all-reduce), kind=kOutput, calls=%fused_computation.19 | convolution fusion | flops 8597274624 | bytes 29374464 | tf_op jit(solution)/shard_map/dot_general | solution.py:30
  315.2 0.0 copy-done
  315.2 0.0 copy-done.3
  315.2 0.0 copy-done.4
  315.2 0.0 copy-done.5
  315.2 4.2 multiply_add_fusion
  319.4 2.5 copy.16
  322.0 2.5 copy.15
  324.5 350.1 %all-reduce.3 = (f32[512]{0:T(512)S(1)}, bf16[512,4096]{1,0:T(8,128)(2,1)}) all-reduce(f32[512]{0:T(512)S(1)} %get-tuple-element.9, f32[512,4096]{1,0:T(8,128)} %fusion.11), channel_id=1, replica_groups=mesh['outer'=4,'vocab'=32] {'vocab'}, use_global_device_ids=true, to_apply=%region_5.0 | all-reduce | flops 2097664 | bytes 12587008 | tf_op jit(solution)/shard_map/psum | solution.py:24
  674.6 0.6 subtract_reduce_fusion
  675.8 1.6 dynamic-slice_convert_fusion
  (2 shorter events, 0.0 us)
Async XLA Ops:
  7.2 4.7 copy-start.1
  7.2 6.0 copy-start.2
  7.2 85.3 %all-gather.2.cloned.1.call-start = ((), (), s32[]{:S(2)}) async-start(), calls=%async_computation | async-start | bytes 4325376 | tf_op jit(solution)/shard_map/all_gather | solution.py:12
  7.9 6.6 copy-start.7
  7.9 7.8 %copy-start.6 = (s32[16]{0:T(128)S(1)}, s32[16]{0:T(128)}, u32[]{:S(2)}) copy-start(s32[16]{0:T(128)} %param.7) | copy-start | bytes 196
  297.0 18.2 %copy-start = (f32[512,2048]{1,0:T(8,128)S(1)}, f32[512,2048]{1,0:T(8,128)}, u32[]{:S(2)}) copy-start(f32[512,2048]{1,0:T(8,128)} %get-tuple-element.15) | copy-start | bytes 12582916
  297.0 18.2 %copy-start.3 = (f32[128,2048]{0,1:T(8,128)S(1)}, f32[128,2048]{0,1:T(8,128)}, u32[]{:S(2)}) copy-start(f32[128,2048]{0,1:T(8,128)} %copy.14) | copy-start | bytes 3145732
  297.0 18.2 %copy-start.4 = (f32[128,2048]{0,1:T(8,128)S(1)}, f32[128,2048]{0,1:T(8,128)}, u32[]{:S(2)}) copy-start(f32[128,2048]{0,1:T(8,128)} %copy.13) | copy-start | bytes 3145732
  297.0 18.2 %copy-start.5 = (f32[128,2048]{0,1:T(8,128)S(1)}, f32[128,2048]{0,1:T(8,128)}, u32[]{:S(2)}) copy-start(f32[128,2048]{0,1:T(8,128)} %copy.12) | copy-start | bytes 3145732
Sparse Core Ops, SparseCore 0:
  11.1 81.3 all-gather.1
where the time goes:
time: 691 us; the launch traced here: 685 us
  blocking collectives  559 us (81%)
  waiting for transfers between devices  55 us (8%)
  matrix products  37.4 us (5%)
  between operations  16.6 us (2%)
  local copies, waits for them, and re-layouts  14 us (2%)
    psum x2, blocking collectives, body(): lax.psum((jnp.sum(jnp.exp(logits - top[:, None]), axis=1), local_pick), '...  445 us
    pmax x1, blocking collectives, body(): top = lax.pmax(local_max, 'vocab')  91.2 us
    all_gather x1, waiting for transfers between devices, body(): lax.all_gather(hidden, 'vocab', axis=0, tiled=True)  54.3 us
    unnamed x1, blocking collectives  22.2 us
    dot_general x1, matrix products, body(): lax.dot_general(dlogits, head, (((1,), (1,)), ((), ())), preferred_elemen...  18.2 us
    dot_general x1, matrix products, body(): logits = jnp.dot(rows_all, head, preferred_element_type=jnp.float32)  15 us
  transfers between devices with their start and end apart: 1, of which 1 were waited for; matrix products, arithmetic and copies ran while one was open for 1% of the time, Pallas kernels for 0%

commit v1 on v0

v1 whole, which is shorter than its diff:
```python
import functools

import jax
import jax.numpy as jnp
from jax import lax
from jax.experimental import pallas as pl
from jax.experimental.pallas import tpu as pltpu
from jax.sharding import PartitionSpec as P

FRAG = 128
REPLICAS = 4
MESH = pl.DeviceIdType.MESH
F32, BF16 = jnp.float32, jnp.bfloat16

NY, NZ, NX = 4, 4, 2
OWN = 16
HALF = NY * NZ * OWN
CHUNK = 1024
EXT = 128
TILE = 512
ORDER = (0, 2, 1, 3)


def kernel(
    hidden_hbm, ext_hbm, head_hbm, global_hbm, momentum_hbm, peer_hbm,
    loss_ref, grad_ref, new_global_hbm, new_momentum_hbm,
    head, g_buf, logits, dl, part, send1, recv1, send2, recv2, summed, recv_a, send_x, recv_x,
    st_y, st_z, st_x, fin, col_top, col_sum, col_pick, fg, mo, pe,
    load_sem, head_sem, frag_sem, out_sem, x_sem, a_sem, b1_sem, b2_sem, st_sem, r1_sem, r2_sem, ra_sem, rx_sem,
):
    outer = lax.axis_index("outer")
    me = lax.axis_index("vocab")
    y, z, xh = me // (NZ * NX), (me // NX) % NZ, me % NX
    width = head.shape[1]
    base = me * width

    def dev(dy=0, dz=0, dx=0):
        return (outer, ((y + dy) % NY) * (NZ * NX) + ((z + dz) % NZ) * NX + (xh + dx) % NX)

    def dev_a(g, d):
        return dev(dy=d) if g == 0 else dev(dz=d)

    def dev_b(g, d):
        return dev(dz=d) if g == 0 else dev(dy=d)

    def at(g, a, b):
        return (a, b) if g == 0 else (b, a)

    def pos(g):
        return (y, z) if g == 0 else (z, y)

    def remote(src, dst, sems, device):
        return pltpu.make_async_remote_copy(
            src_ref=src, dst_ref=dst, send_sem=sems.at[0], recv_sem=sems.at[1], device_id=device, device_id_type=MESH
        )

    sent = []

    def go(copies):
        for copy in copies:
            copy.start()
            sent.append(copy)
        return copies

    def arrived(copies):
        for copy in copies:
            copy.wait_recv()

    loads = [
        pltpu.make_async_copy(hidden_hbm, g_buf.at[xh, y, z, :, pl.ds(0, 4 * CHUNK)], load_sem.at[0]),
        pltpu.make_async_copy(ext_hbm, g_buf.at[xh, y, z, :, pl.ds(4 * CHUNK, EXT)], load_sem.at[1]),
    ]
    for copy in loads:
        copy.start()
    head_loads = {}
    for c in ORDER:
        rows = pl.ds(c * CHUNK, CHUNK)
        head_loads[c] = pltpu.make_async_copy(head_hbm.at[rows], head.at[rows], head_sem.at[c])
        head_loads[c].start()
    frag_loads = [
        pltpu.make_async_copy(src, dst, frag_sem.at[i])
        for i, (src, dst) in enumerate(((global_hbm, fg), (momentum_hbm, mo), (peer_hbm, pe)))
    ]
    for copy in frag_loads:
        copy.start()

    barrier = pltpu.get_barrier_semaphore()
    partners = [dev(dy=1), dev(dy=2), dev(dy=3), dev(dz=1), dev(dz=2), dev(dz=3), dev(dx=1)]
    for partner in partners:
        pl.semaphore_signal(barrier, inc=1, device_id=partner, device_id_type=MESH)
    pl.semaphore_wait(barrier, len(partners))

    def columns(c):
        return pl.ds(c * CHUNK, CHUNK + (EXT if c == 3 else 0))

    for copy in loads:
        copy.wait()
    swap = go([remote(g_buf.at[xh, y, z], g_buf.at[xh, y, z], x_sem, dev(dx=1))])

    def gather_a(h):
        copies = []
        for g in range(2):
            cols = pl.ds(2 * CHUNK * g, 2 * CHUNK + (EXT if g == 1 else 0))
            block = g_buf.at[h, y, z, :, cols]
            copies += [remote(block, block, a_sem.at[h, g, d - 1], dev_a(g, d)) for d in (1, 2, 3)]
        return go(copies)

    def gather_b1(h, c):
        g = c // 2
        b = pos(g)[1]
        block = g_buf.at[(h, *at(g, slice(None), b), slice(None), columns(c))]
        return go([remote(block, block, b1_sem.at[h, c, i], dev_b(g, d)) for i, d in enumerate((1, 3))])

    def gather_b2(h, c, first):
        g = c // 2
        b = pos(g)[1]
        copies = []
        for i, d in enumerate((1, 3)):
            first[i].wait_recv()
            block = g_buf.at[(h, *at(g, slice(2 * i, 2 * i + 2), (b + 4 - d) % 4), slice(None), columns(c))]
            copies += go([remote(block, block, b2_sem.at[h, c, i], dev_b(g, d))])
        return copies

    def forward(h, c, second):
        arrived(second)
        if h == 0:
            head_loads[c].wait()
        lo = c * CHUNK

        @pl.loop(0, width // TILE)
        def _(j):
            cols = pl.ds(pl.multiple_of(j * TILE, TILE), TILE)
            rows = g_buf[h, :, :, :, lo : lo + CHUNK].reshape(HALF, CHUNK)
            out = jnp.dot(rows, head[lo : lo + CHUNK, cols], preferred_element_type=F32)
            if c == ORDER[0]:
                logits[h, :, cols] = out
            else:
                logits[h, :, cols] = logits[h, :, cols] + out

    eye = lax.broadcasted_iota(jnp.int32, (128, 128), 0) == lax.broadcasted_iota(jnp.int32, (128, 128), 1)

    def to_lanes(ref, i):
        return jnp.sum(jnp.where(eye, ref[128 * i : 128 * (i + 1), :], 0.0), axis=0, keepdims=True)

    STEP = 32

    def target_columns(h, i):
        t = g_buf[h, i // 2, pl.ds((i % 2) * 2, 2), :, 4 * CHUNK : 4 * CHUNK + EXT]
        t = t.reshape(STEP, EXT).astype(F32)
        return (t[:, 0:1] * 256.0 + t[:, 1:2]).astype(jnp.int32) - base

    def softmax_local(h):
        @pl.loop(0, HALF // STEP)
        def _(i):
            rows = pl.ds(pl.multiple_of(i * STEP, STEP), STEP)
            values = logits[h, rows, :]
            target = target_columns(h, i)
            column = lax.broadcasted_iota(jnp.int32, (STEP, width), 1)
            top = jnp.max(values, axis=1, keepdims=True)
            shifted = jnp.exp(values - top)
            logits[h, rows, :] = shifted
            col_top[h, rows, :] = jnp.broadcast_to(top, (STEP, 128))
            col_sum[rows, :] = jnp.broadcast_to(jnp.sum(shifted, axis=1, keepdims=True), (STEP, 128))
            picked = jnp.sum(jnp.where(column == target, values, 0.0), axis=1, keepdims=True)
            col_pick[rows, :] = jnp.broadcast_to(picked, (STEP, 128))

    def stat_send(h, stage):
        if stage == 0:
            slot = st_y.at[h, y]
            copies = [remote(slot, slot, st_sem.at[h, d - 1], dev(dy=d)) for d in (1, 2, 3)]
        elif stage == 1:
            slot = st_z.at[h, z]
            copies = [remote(slot, slot, st_sem.at[h, 2 + d], dev(dz=d)) for d in (1, 2, 3)]
        else:
            slot = st_x.at[h, xh]
            copies = [remote(slot, slot, st_sem.at[h, 6], dev(dx=1))]
        return go(copies)

    def stats_start(h):
        tile = [to_lanes(col_top.at[h], i) for i in range(2)]
        tile += [to_lanes(ref, i) for ref in (col_sum, col_pick) for i in range(2)]
        tile += [jnp.zeros((2, 128), F32)]
        st_y[h, y] = jnp.concatenate(tile, axis=0)
        return stat_send(h, 0)

    def combine(ref, h, n):
        tops = [ref[h, i, 0:2, :] for i in range(n)]
        top = functools.reduce(jnp.maximum, tops)
        total = sum(ref[h, i, 2:4, :] * jnp.exp(tops[i] - top) for i in range(n))
        picked = sum(ref[h, i, 4:6, :] for i in range(n))
        return jnp.concatenate([top, total, picked, jnp.zeros((2, 128), F32)], axis=0)

    def stats_next(h, stage, copies):
        arrived(copies)
        if stage == 1:
            st_z[h, z] = combine(st_y, h, NY)
        else:
            st_x[h, xh] = combine(st_z, h, NZ)
        return stat_send(h, stage)

    def stats_end(h, copies):
        arrived(copies)
        fin[h] = combine(st_x, h, NX)

    def gradient_logits(h):
        row_count = NX * HALF
        for i in range(2):
            top = jnp.broadcast_to(fin[h, i : i + 1, :], (128, 128))
            total = jnp.broadcast_to(fin[h, 2 + i : 3 + i, :], (128, 128))
            top = jnp.sum(jnp.where(eye, top, 0.0), axis=1, keepdims=True)
            total = jnp.sum(jnp.where(eye, total, 0.0), axis=1, keepdims=True)
            scale = jnp.exp(col_top[h, 128 * i : 128 * (i + 1), :] - top) / (total * row_count)
            col_sum[128 * i : 128 * (i + 1), :] = scale

        @pl.loop(0, HALF // STEP)
        def _(i):
            rows = pl.ds(pl.multiple_of(i * STEP, STEP), STEP)
            target = target_columns(h, i)
            column = lax.broadcasted_iota(jnp.int32, (STEP, width), 1)
            scale = col_sum[rows, 0:1]
            onehot = jnp.where(column == target, 1.0 / row_count, 0.0)
            dl[h, rows, :] = (logits[h, rows, :] * scale - onehot).astype(BF16)

    def piece(k):
        h, c = k // 4, ORDER[k % 4]
        g = c // 2
        a, b = pos(g)
        return h, c, g, a, b

    def backward(k):
        h, c, g, a, b = piece(k)

        @pl.loop(0, CHUNK // TILE)
        def _(j):
            rows = pl.ds(pl.multiple_of(c * CHUNK + j * TILE, TILE), TILE)
            cols = pl.ds(pl.multiple_of(j * TILE, TILE), TILE)
            out = lax.dot_general(dl[h], head[rows, :], (((1,), (1,)), ((), ())), preferred_element_type=F32)
            part[k, :, :, :, cols] = out.reshape(NY, NZ, OWN, TILE)

        def own(d, first):
            return part[(k, *at(g, slice(first, first + 2), (b + d) % 4))]

        send1[k, 0, 0:2] = own(2, 0).astype(BF16)
        send1[k, 0, 2:4] = own(1, 2).astype(BF16)
        send1[k, 1, 0:2] = own(3, 0).astype(BF16)
        send1[k, 1, 2:4] = own(2, 2).astype(BF16)
        return go(
            [remote(send1.at[k, i], recv1.at[k, i], r1_sem.at[k, i], dev_b(g, d)) for i, d in enumerate((1, 3))]
        )

    def reduce_b(k, first):
        h, c, g, a, b = piece(k)
        copies = []
        for i, d in enumerate((1, 3)):
            first[i].wait_recv()
            mine = part[(k, *at(g, slice(2 * i, 2 * i + 2), (b + d) % 4))]
            send2[k, i] = (mine + recv1[k, i, 2 * i : 2 * i + 2].astype(F32)).astype(BF16)
            copies += go([remote(send2.at[k, i], recv2.at[k, i], r2_sem.at[k, i], dev_b(g, d))])
        return copies

    def reduce_a(k, second):
        h, c, g, a, b = piece(k)
        arrived(second)
        for i in range(2):
            mine = part[(k, *at(g, slice(2 * i, 2 * i + 2), b))]
            near = recv1[k, 1 - i, 2 * i : 2 * i + 2].astype(F32)
            summed[k, 2 * i : 2 * i + 2] = mine + near + recv2[k, i].astype(F32)
        return go(
            [
                remote(summed.at[k, (a + d) % 4], recv_a.at[k, d - 1], ra_sem.at[k, d - 1], dev_a(g, d))
                for d in (1, 2, 3)
            ]
        )

    def reduce_x(k, copies):
        h, c, g, a, b = piece(k)
        arrived(copies)
        send_x[k] = summed[k, a] + recv_a[k, 0] + recv_a[k, 1] + recv_a[k, 2]
        copy = remote(send_x.at[k], recv_x.at[k % 4], rx_sem.at[k % 4], dev(dx=1))

        @pl.when(xh != h)
        def _():
            copy.start()

    def finish():
        for k in range(8):
            h, c, g, a, b = piece(k)
            copy = remote(send_x.at[k], recv_x.at[k % 4], rx_sem.at[k % 4], dev(dx=1))

            @pl.when(xh != h)
            def _():
                copy.wait_send()

            @pl.when(xh == h)
            def _():
                copy.wait_recv()
                grad_ref[:, c * CHUNK : (c + 1) * CHUNK] = (send_x[k] + recv_x[k % 4]).astype(BF16)

    def fragment():
        for copy in frag_loads:
            copy.wait()
        rows = g_buf[:, :, :, :, 0:FRAG].reshape(NX * HALF, FRAG)
        turned = rows.astype(F32).T.astype(BF16)

        @pl.loop(0, width // TILE)
        def _(j):
            cols = pl.ds(pl.multiple_of(j * TILE, TILE), TILE)
            grad = sum(
                jnp.dot(turned[:, h * HALF : (h + 1) * HALF], dl[h, :, cols], preferred_element_type=F32)
                for h in range(NX)
            )
            local = head[0:FRAG, cols].astype(F32) - 1.0 * grad
            outer_value = fg[:, cols]
            pseudo = (outer_value - local + pe[:, cols]) / REPLICAS
            momentum = 0.9 * mo[:, cols] + pseudo
            mo[:, cols] = momentum
            fg[:, cols] = outer_value - 0.7 * (pseudo + 0.9 * momentum)

        stores = [
            pltpu.make_async_copy(fg, new_global_hbm, out_sem.at[0]),
            pltpu.make_async_copy(mo, new_momentum_hbm, out_sem.at[1]),
        ]
        for copy in stores:
            copy.start()
        return stores

    def loss():
        terms = sum(fin[h, 0:2, :] + jnp.log(fin[h, 2:4, :]) - fin[h, 4:6, :] for h in range(NX))
        loss_ref[0] = jnp.sum(terms) / (NX * HALF)

    arrived(swap)
    a0 = gather_a(0)
    arrived(a0)
    b1 = {(0, c): gather_b1(0, c) for c in ORDER[:2]}
    a1 = gather_a(1)
    b1.update({(0, c): gather_b1(0, c) for c in ORDER[2:]})
    b2 = {(0, c): gather_b2(0, c, b1[0, c]) for c in ORDER[:2]}
    arrived(a1)
    b1.update({(1, c): gather_b1(1, c) for c in ORDER[:2]})
    b2.update({(0, c): gather_b2(0, c, b1[0, c]) for c in ORDER[2:]})
    forward(0, 0, b2[0, 0])
    b1.update({(1, c): gather_b1(1, c) for c in ORDER[2:]})
    forward(0, 2, b2[0, 2])
    b2.update({(1, c): gather_b2(1, c, b1[1, c]) for c in ORDER[:2]})
    forward(0, 1, b2[0, 1])
    forward(0, 3, b2[0, 3])
    softmax_local(0)
    s = stats_start(0)
    b2.update({(1, c): gather_b2(1, c, b1[1, c]) for c in ORDER[2:]})
    forward(1, 0, b2[1, 0])
    s = stats_next(0, 1, s)
    forward(1, 2, b2[1, 2])
    s = stats_next(0, 2, s)
    forward(1, 1, b2[1, 1])
    stats_end(0, s)
    gradient_logits(0)
    r = {0: backward(0)}
    forward(1, 3, b2[1, 3])
    r[1] = backward(1)
    r[0] = reduce_b(0, r[0])
    softmax_local(1)
    s = stats_start(1)
    r[1] = reduce_b(1, r[1])
    r[0] = reduce_a(0, r[0])
    r[2] = backward(2)
    s = stats_next(1, 1, s)
    r[1] = reduce_a(1, r[1])
    reduce_x(0, r[0])
    r[2] = reduce_b(2, r[2])
    r[3] = backward(3)
    s = stats_next(1, 2, s)
    reduce_x(1, r[1])
    r[3] = reduce_b(3, r[3])
    r[2] = reduce_a(2, r[2])
    stats_end(1, s)
    gradient_logits(1)
    r[4] = backward(4)
    r[3] = reduce_a(3, r[3])
    reduce_x(2, r[2])
    r[5] = backward(5)
    r[4] = reduce_b(4, r[4])
    reduce_x(3, r[3])
    r[6] = backward(6)
    r[5] = reduce_b(5, r[5])
    r[4] = reduce_a(4, r[4])
    r[7] = backward(7)
    r[6] = reduce_b(6, r[6])
    r[5] = reduce_a(5, r[5])
    reduce_x(4, r[4])
    stores = fragment()
    loss()
    r[7] = reduce_b(7, r[7])
    r[6] = reduce_a(6, r[6])
    reduce_x(5, r[5])
    r[7] = reduce_a(7, r[7])
    reduce_x(6, r[6])
    reduce_x(7, r[7])
    finish()
    for copy in sent:
        copy.wait_send()
    for copy in stores:
        copy.wait()


def body(hidden, targets, head, global_frag, momentum, peer_delta):
    own, depth = hidden.shape
    width = head.shape[1]
    digits = jnp.stack([targets // 256, targets % 256], axis=1).astype(BF16)
    ext = jnp.pad(digits, ((0, 0), (0, EXT - 2)))
    dma = pltpu.SemaphoreType.DMA
    pieces = 8
    loss, grad, new_global, new_momentum = pl.pallas_call(
        kernel,
        out_shape=(
            jax.ShapeDtypeStruct((1,), F32),
            jax.ShapeDtypeStruct((own, depth), BF16),
            jax.ShapeDtypeStruct((FRAG, width), F32),
            jax.ShapeDtypeStruct((FRAG, width), F32),
        ),
        in_specs=[pl.BlockSpec(memory_space=pl.ANY)] * 6,
        out_specs=(
            pl.BlockSpec(memory_space=pltpu.SMEM),
            pl.BlockSpec(memory_space=pltpu.VMEM),
            pl.BlockSpec(memory_space=pl.ANY),
            pl.BlockSpec(memory_space=pl.ANY),
        ),
        scratch_shapes=[
            pltpu.VMEM((depth, width), BF16),
            pltpu.VMEM((NX, NY, NZ, OWN, depth + EXT), BF16),
            pltpu.VMEM((NX, HALF, width), F32),
            pltpu.VMEM((NX, HALF, width), BF16),
            pltpu.VMEM((pieces, NY, NZ, OWN, CHUNK), F32),
            pltpu.VMEM((pieces, 2, 4, OWN, CHUNK), BF16),
            pltpu.VMEM((pieces, 2, 4, OWN, CHUNK), BF16),
            pltpu.VMEM((pieces, 2, 2, OWN, CHUNK), BF16),
            pltpu.VMEM((pieces, 2, 2, OWN, CHUNK), BF16),
            pltpu.VMEM((pieces, 4, OWN, CHUNK), F32),
            pltpu.VMEM((pieces, 3, OWN, CHUNK), F32),
            pltpu.VMEM((pieces, OWN, CHUNK), F32),
            pltpu.VMEM((4, OWN, CHUNK), F32),
            pltpu.VMEM((NX, NY, 8, 128), F32),
            pltpu.VMEM((NX, NZ, 8, 128), F32),
            pltpu.VMEM((NX, NX, 8, 128), F32),
            pltpu.VMEM((NX, 8, 128), F32),
            pltpu.VMEM((NX, HALF, 128), F32),
            pltpu.VMEM((HALF, 128), F32),
            pltpu.VMEM((HALF, 128), F32),
            pltpu.VMEM((FRAG, width), F32),
            pltpu.VMEM((FRAG, width), F32),
            pltpu.VMEM((FRAG, width), F32),
            dma((2,)),
            dma((4,)),
            dma((3,)),
            dma((2,)),
            dma((2,)),
            dma((2, 2, 3, 2)),
            dma((2, 4, 2, 2)),
            dma((2, 4, 2, 2)),
            dma((2, 7, 2)),
            dma((pieces, 2, 2)),
            dma((pieces, 2, 2)),
            dma((pieces, 3, 2)),
            dma((4, 2)),
        ],
        compiler_params=pltpu.CompilerParams(
            collective_id=0, has_side_effects=True, vmem_limit_bytes=62 << 20
        ),
        cost_estimate=pl.CostEstimate(flops=18 * 10**9, bytes_accessed=24 * 2**20, transcendentals=2**20),
    )(hidden, ext, head, global_frag, momentum, peer_delta)
    return loss, grad, new_global, new_momentum


def solution(mesh):
    in_specs = (
        P(("outer", "vocab"), None),
        P(("outer", "vocab")),
        P("outer", "vocab"),
        P(None, "vocab"),
        P(None, "vocab"),
        P("outer", "vocab"),
    )
    out_specs = (P("outer"), P(("outer", "vocab"), None), P("outer", "vocab"), P("outer", "vocab"))
    return jax.shard_map(body, mesh=mesh, in_specs=in_specs, out_specs=out_specs, check_vma=False)
```

time: 691 us -> 123 us (0.18)
  blocking collectives: 559 us -> 0 us
  Pallas kernels: 0 us -> 112 us
  waiting for transfers between devices: 55 us -> 0 us
  matrix products: 37.4 us -> 0 us
  between operations: 16.6 us -> 2.39 us
  local copies, waits for them, and re-layouts: 14 us -> 6.86 us
    psum x2 -> x0, blocking collectives: 445 us -> none  [body(): lax.psum((jnp.sum(jnp.exp(logits - top[:, None]), axis=1), local_pick), '...]
    pallas_call x0 -> x1, Pallas kernels: none -> 112 us  [body(): pl.pallas_call(kernel, out_shape=(jax.ShapeDtypeStruct((1,), F32), jax.Sh...]
    pmax x1 -> x0, blocking collectives: 91.2 us -> none  [body(): top = lax.pmax(local_max, 'vocab')]
    all_gather x1 -> x0, waiting for transfers between devices: 54.3 us -> none  [body(): lax.all_gather(hidden, 'vocab', axis=0, tiled=True)]
    dot_general x3 -> x0, matrix products: 37.4 us -> none  [the longest x1 18.2 us: body(): lax.dot_general(dlogits, head, (((1,), (1,)), ((), ())), preferred_elemen...]
    unnamed x1 -> x0, blocking collectives: 22.2 us -> none
  transfers between devices with their start and end apart: 1 -> 0, of which waited for: 1 -> 0; matrix products, arithmetic and copies ran while one was open for 1% -> 0% of each run, Pallas kernels for 0% -> 0%
where the time goes in v1:
time: 123 us; the launch traced here: 122 us
  Pallas kernels  112 us (91%)
  local copies, waits for them, and re-layouts  6.86 us (6%)
  between operations  2.39 us (2%)
    pallas_call x1, Pallas kernels, body(): pl.pallas_call(kernel, out_shape=(jax.ShapeDtypeStruct((1,), F32), jax.Sh...  112 us
    unnamed x3, local copies, waits for them, and re-layouts  6.16 us

profile of v1, /device:TPU:6, one launch (start us, length us, event | category | flops | bytes accessed | tf_op | source)
XLA Modules:
  0.0 122.4 jit_solution(1467462909442913847)
XLA Ops:
  0.6 0.7 convert_bitcast_fusion
  1.3 0.1 copy.12
  1.4 0.6 pad.4.ext_hbm
  2.0 112.4 %shard_map.93 = (f32[1]{0:T(128)}, bf16[16,4096]{1,0:T(8,128)(2,1)}, f32[128,2048]{1,0:T(8,128)}, f32[128,2048]{1,0:T(8,128)}) custom-call(bf16[16,4096]{1,0:T(8,128)(2,1)} %hidden_hbm.1, bf16[16,128]{1,0:T(8,128)(2,1)} %pad.4.ext_hbm, bf16[4096,2048]{1,0:T(8,128)(2,1)} %head_hbm.1, f32[128,2048]{1,0:T(8,128)} %global_hbm.1, f32[128,2048]{1,0:T(8,128)} %momentum_hbm.1, ...), custom_call_target="tpu_custom_call" | custom-call | flops 17999998976 | bytes 25165824 | tf_op jit(solution)/shard_map/pallas_call | solution.py:412
  115.1 1.6 %copy.18 = bf16[16,4096]{1,0:T(8,128)(2,1)} copy(bf16[16,4096]{1,0:T(8,128)(2,1)} %get-tuple-element.11) | data formatting | bytes 262144
  116.7 2.3 %copy.19 = f32[128,2048]{1,0:T(8,128)} copy(f32[128,2048]{1,0:T(8,128)} %get-tuple-element.12) | data formatting | bytes 2097152
  118.9 2.3 %copy.20 = f32[128,2048]{1,0:T(8,128)} copy(f32[128,2048]{1,0:T(8,128)} %get-tuple-element.13) | data formatting | bytes 2097152
  (1 shorter events, 0.0 us)

commit v2 on v1

--- a/solution.py
+++ b/solution.py
@@ -18,14 +18,15 @@
 CHUNK = 1024
 EXT = 128
 TILE = 512
+PARTS = 4
 ORDER = (0, 2, 1, 3)
 
 
 def kernel(
-    hidden_hbm, ext_hbm, head_hbm, global_hbm, momentum_hbm, peer_hbm,
+    targets_ref, hidden_hbm, head_hbm, global_hbm, momentum_hbm, peer_hbm,
     loss_ref, grad_ref, new_global_hbm, new_momentum_hbm,
     head, g_buf, logits, dl, part, send1, recv1, send2, recv2, summed, recv_a, send_x, recv_x,
-    st_y, st_z, st_x, fin, col_top, col_sum, col_pick, fg, mo, pe,
+    st_plane, st_z, fin, col_top, col_sum, col_pick, fg, mo, pe,
     load_sem, head_sem, frag_sem, out_sem, x_sem, a_sem, b1_sem, b2_sem, st_sem, r1_sem, r2_sem, ra_sem, rx_sem,
 ):
     outer = lax.axis_index("outer")
@@ -66,12 +67,8 @@
         for copy in copies:
             copy.wait_recv()
 
-    loads = [
-        pltpu.make_async_copy(hidden_hbm, g_buf.at[xh, y, z, :, pl.ds(0, 4 * CHUNK)], load_sem.at[0]),
-        pltpu.make_async_copy(ext_hbm, g_buf.at[xh, y, z, :, pl.ds(4 * CHUNK, EXT)], load_sem.at[1]),
-    ]
-    for copy in loads:
-        copy.start()
+    load = pltpu.make_async_copy(hidden_hbm, g_buf.at[xh, y, z, :, pl.ds(0, 4 * CHUNK)], load_sem)
+    load.start()
     head_loads = {}
     for c in ORDER:
         rows = pl.ds(c * CHUNK, CHUNK)
@@ -85,57 +82,65 @@
         copy.start()
 
     barrier = pltpu.get_barrier_semaphore()
-    partners = [dev(dy=1), dev(dy=2), dev(dy=3), dev(dz=1), dev(dz=2), dev(dz=3), dev(dx=1)]
+    plane = [(dx, dy) for dx in range(NX) for dy in range(NY) if dx or dy]
+    partners = [dev(dz=d) for d in (1, 2, 3)] + [dev(dx=dx, dy=dy) for dx, dy in plane]
     for partner in partners:
         pl.semaphore_signal(barrier, inc=1, device_id=partner, device_id_type=MESH)
+
+    row = lax.broadcasted_iota(jnp.int32, (OWN, EXT), 0)
+    lane = lax.broadcasted_iota(jnp.int32, (OWN, EXT), 1)
+    digits = jnp.zeros((OWN, EXT), jnp.int32)
+    for i in range(OWN):
+        target = targets_ref[i]
+        digits = jnp.where(row == i, jnp.where(lane == 0, target >> 8, target & 255), digits)
+    g_buf[xh, y, z, :, 4 * CHUNK : 4 * CHUNK + EXT] = digits.astype(F32).astype(BF16)
     pl.semaphore_wait(barrier, len(partners))
 
     def columns(c):
         return pl.ds(c * CHUNK, CHUNK + (EXT if c == 3 else 0))
 
-    for copy in loads:
-        copy.wait()
-    swap = go([remote(g_buf.at[xh, y, z], g_buf.at[xh, y, z], x_sem, dev(dx=1))])
-
-    def gather_a(h):
-        copies = []
-        for g in range(2):
-            cols = pl.ds(2 * CHUNK * g, 2 * CHUNK + (EXT if g == 1 else 0))
-            block = g_buf.at[h, y, z, :, cols]
-            copies += [remote(block, block, a_sem.at[h, g, d - 1], dev_a(g, d)) for d in (1, 2, 3)]
-        return go(copies)
+    load.wait()
+
+    def swap_x(c):
+        block = g_buf.at[xh, y, z, :, columns(c)]
+        return go([remote(block, block, x_sem.at[c], dev(dx=1))])
+
+    def gather_a(h, c):
+        block = g_buf.at[h, y, z, :, columns(c)]
+        return [remote(block, block, a_sem.at[h, c, d - 1], dev_a(c // 2, d)) for d in (1, 2, 3)]
 
     def gather_b1(h, c):
         g = c // 2
         b = pos(g)[1]
-        block = g_buf.at[(h, *at(g, slice(None), b), slice(None), columns(c))]
-        return go([remote(block, block, b1_sem.at[h, c, i], dev_b(g, d)) for i, d in enumerate((1, 3))])
+        copies = [[None, None], [None, None]]
+        for p in range(2):
+            for i, d in enumerate((1, 3)):
+                q = p if i == 0 else 1 - p
+                block = g_buf.at[(h, *at(g, slice(2 * q, 2 * q + 2), b), slice(None), columns(c))]
+                (copies[i][q],) = go([remote(block, block, b1_sem.at[h, c, i, q], dev_b(g, d))])
+        return copies
 
     def gather_b2(h, c, first):
         g = c // 2
         b = pos(g)[1]
         copies = []
         for i, d in enumerate((1, 3)):
-            first[i].wait_recv()
+            first[i][i].wait_recv()
             block = g_buf.at[(h, *at(g, slice(2 * i, 2 * i + 2), (b + 4 - d) % 4), slice(None), columns(c))]
             copies += go([remote(block, block, b2_sem.at[h, c, i], dev_b(g, d))])
-        return copies
+        return copies + [first[0][1], first[1][0]]
 
     def forward(h, c, second):
         arrived(second)
         if h == 0:
             head_loads[c].wait()
         lo = c * CHUNK
-
-        @pl.loop(0, width // TILE)
-        def _(j):
-            cols = pl.ds(pl.multiple_of(j * TILE, TILE), TILE)
-            rows = g_buf[h, :, :, :, lo : lo + CHUNK].reshape(HALF, CHUNK)
-            out = jnp.dot(rows, head[lo : lo + CHUNK, cols], preferred_element_type=F32)
-            if c == ORDER[0]:
-                logits[h, :, cols] = out
-            else:
-                logits[h, :, cols] = logits[h, :, cols] + out
+        rows = g_buf[h, :, :, :, lo : lo + CHUNK].reshape(HALF, CHUNK)
+        out = jnp.dot(rows, head[lo : lo + CHUNK, :], preferred_element_type=F32)
+        if c == ORDER[0]:
+            logits[h] = out
+        else:
+            logits[h] = logits[h] + out
 
     eye = lax.broadcasted_iota(jnp.int32, (128, 128), 0) == lax.broadcasted_iota(jnp.int32, (128, 128), 1)
 
@@ -166,41 +171,35 @@
 
     def stat_send(h, stage):
         if stage == 0:
-            slot = st_y.at[h, y]
-            copies = [remote(slot, slot, st_sem.at[h, d - 1], dev(dy=d)) for d in (1, 2, 3)]
-        elif stage == 1:
+            slot = st_plane.at[h, xh, y]
+            copies = [remote(slot, slot, st_sem.at[h, dx * NY + dy - 1], dev(dx=dx, dy=dy)) for dx, dy in plane]
+        else:
             slot = st_z.at[h, z]
-            copies = [remote(slot, slot, st_sem.at[h, 2 + d], dev(dz=d)) for d in (1, 2, 3)]
-        else:
-            slot = st_x.at[h, xh]
-            copies = [remote(slot, slot, st_sem.at[h, 6], dev(dx=1))]
+            copies = [remote(slot, slot, st_sem.at[h, 6 + d], dev(dz=d)) for d in (1, 2, 3)]
         return go(copies)
 
     def stats_start(h):
         tile = [to_lanes(col_top.at[h], i) for i in range(2)]
         tile += [to_lanes(ref, i) for ref in (col_sum, col_pick) for i in range(2)]
         tile += [jnp.zeros((2, 128), F32)]
-        st_y[h, y] = jnp.concatenate(tile, axis=0)
+        st_plane[h, xh, y] = jnp.concatenate(tile, axis=0)
         return stat_send(h, 0)
 
-    def combine(ref, h, n):
-        tops = [ref[h, i, 0:2, :] for i in range(n)]
+    def combine(tiles):
+        tops = [tile[0:2] for tile in tiles]
         top = functools.reduce(jnp.maximum, tops)
-        total = sum(ref[h, i, 2:4, :] * jnp.exp(tops[i] - top) for i in range(n))
-        picked = sum(ref[h, i, 4:6, :] for i in range(n))
+        total = sum(tile[2:4] * jnp.exp(tile[0:2] - top) for tile in tiles)
+        picked = sum(tile[4:6] for tile in tiles)
         return jnp.concatenate([top, total, picked, jnp.zeros((2, 128), F32)], axis=0)
 
-    def stats_next(h, stage, copies):
+    def stats_next(h, copies):
         arrived(copies)
-        if stage == 1:
-            st_z[h, z] = combine(st_y, h, NY)
-        else:
-            st_x[h, xh] = combine(st_z, h, NZ)
-        return stat_send(h, stage)
+        st_z[h, z] = combine([st_plane[h, i, j] for i in range(NX) for j in range(NY)])
+        return stat_send(h, 1)
 
     def stats_end(h, copies):
         arrived(copies)
-        fin[h] = combine(st_x, h, NX)
+        fin[h] = combine([st_z[h, i] for i in range(NZ)])
 
     def gradient_logits(h):
         row_count = NX * HALF
@@ -230,33 +229,38 @@
     def backward(k):
         h, c, g, a, b = piece(k)
 
-        @pl.loop(0, CHUNK // TILE)
-        def _(j):
-            rows = pl.ds(pl.multiple_of(c * CHUNK + j * TILE, TILE), TILE)
-            cols = pl.ds(pl.multiple_of(j * TILE, TILE), TILE)
-            out = lax.dot_general(dl[h], head[rows, :], (((1,), (1,)), ((), ())), preferred_element_type=F32)
-            part[k, :, :, :, cols] = out.reshape(NY, NZ, OWN, TILE)
+        out = lax.dot_general(
+            dl[h], head[c * CHUNK : (c + 1) * CHUNK, :], (((1,), (1,)), ((), ())), preferred_element_type=F32
+        )
+        part[k] = out.reshape(NY, NZ, OWN, CHUNK)
 
         def own(d, first):
             return part[(k, *at(g, slice(first, first + 2), (b + d) % 4))]
 
         send1[k, 0, 0:2] = own(2, 0).astype(BF16)
-        send1[k, 0, 2:4] = own(1, 2).astype(BF16)
-        send1[k, 1, 0:2] = own(3, 0).astype(BF16)
         send1[k, 1, 2:4] = own(2, 2).astype(BF16)
-        return go(
-            [remote(send1.at[k, i], recv1.at[k, i], r1_sem.at[k, i], dev_b(g, d)) for i, d in enumerate((1, 3))]
-        )
+        copies = [[None, None], [None, None]]
+        for p in range(2):
+            if p == 1:
+                send1[k, 0, 2:4] = own(1, 2).astype(BF16)
+                send1[k, 1, 0:2] = own(3, 0).astype(BF16)
+            for i, d in enumerate((1, 3)):
+                q = p if i == 0 else 1 - p
+                half = pl.ds(2 * q, 2)
+                (copies[i][q],) = go(
+                    [remote(send1.at[k, i, half], recv1.at[k, i, half], r1_sem.at[k, i, q], dev_b(g, d))]
+                )
+        return copies
 
     def reduce_b(k, first):
         h, c, g, a, b = piece(k)
         copies = []
         for i, d in enumerate((1, 3)):
-            first[i].wait_recv()
+            first[i][i].wait_recv()
             mine = part[(k, *at(g, slice(2 * i, 2 * i + 2), (b + d) % 4))]
             send2[k, i] = (mine + recv1[k, i, 2 * i : 2 * i + 2].astype(F32)).astype(BF16)
             copies += go([remote(send2.at[k, i], recv2.at[k, i], r2_sem.at[k, i], dev_b(g, d))])
-        return copies
+        return copies + [first[0][1], first[1][0]]
 
     def reduce_a(k, second):
         h, c, g, a, b = piece(k)
@@ -328,69 +332,70 @@
         terms = sum(fin[h, 0:2, :] + jnp.log(fin[h, 2:4, :]) - fin[h, 4:6, :] for h in range(NX))
         loss_ref[0] = jnp.sum(terms) / (NX * HALF)
 
-    arrived(swap)
-    a0 = gather_a(0)
-    arrived(a0)
-    b1 = {(0, c): gather_b1(0, c) for c in ORDER[:2]}
-    a1 = gather_a(1)
-    b1.update({(0, c): gather_b1(0, c) for c in ORDER[2:]})
-    b2 = {(0, c): gather_b2(0, c, b1[0, c]) for c in ORDER[:2]}
-    arrived(a1)
-    b1.update({(1, c): gather_b1(1, c) for c in ORDER[:2]})
-    b2.update({(0, c): gather_b2(0, c, b1[0, c]) for c in ORDER[2:]})
-    forward(0, 0, b2[0, 0])
-    b1.update({(1, c): gather_b1(1, c) for c in ORDER[2:]})
-    forward(0, 2, b2[0, 2])
-    b2.update({(1, c): gather_b2(1, c, b1[1, c]) for c in ORDER[:2]})
-    forward(0, 1, b2[0, 1])
-    forward(0, 3, b2[0, 3])
+    C0, C1, C2, C3 = ORDER
+    xs = {c: swap_x(c) for c in ORDER}
+    go(gather_a(xh, C0) + gather_a(xh, C1))
+    for c in (C0, C1): arrived(xs[c]); go(gather_a(1 - xh, c))
+    b1 = {}
+    b2 = {}
+    for c in (C0, C1): arrived(gather_a(0, c)); b1[0, c] = gather_b1(0, c)
+    go(gather_a(xh, C2) + gather_a(xh, C3))
+    for c in (C2, C3): arrived(xs[c]); go(gather_a(1 - xh, c))
+    for c in (C0, C1): b2[0, c] = gather_b2(0, c, b1[0, c])
+    for c in (C2, C3): arrived(gather_a(0, c)); b1[0, c] = gather_b1(0, c)
+    forward(0, C0, b2[0, C0])
+    for c in (C0, C1): arrived(gather_a(1, c)); b1[1, c] = gather_b1(1, c)
+    for c in (C2, C3): b2[0, c] = gather_b2(0, c, b1[0, c])
+    forward(0, C1, b2[0, C1])
+    for c in (C2, C3): arrived(gather_a(1, c)); b1[1, c] = gather_b1(1, c)
+    for c in (C0, C1): b2[1, c] = gather_b2(1, c, b1[1, c])
+    forward(0, C2, b2[0, C2])
+    forward(0, C3, b2[0, C3])
     softmax_local(0)
     s = stats_start(0)
-    b2.update({(1, c): gather_b2(1, c, b1[1, c]) for c in ORDER[2:]})
-    forward(1, 0, b2[1, 0])
-    s = stats_next(0, 1, s)
-    forward(1, 2, b2[1, 2])
-    s = stats_next(0, 2, s)
-    forward(1, 1, b2[1, 1])
+    for c in (C2, C3): b2[1, c] = gather_b2(1, c, b1[1, c])
+    forward(1, C0, b2[1, C0])
+    forward(1, C1, b2[1, C1])
+    s = stats_next(0, s)
+    forward(1, C2, b2[1, C2])
     stats_end(0, s)
     gradient_logits(0)
     r = {0: backward(0)}
-    forward(1, 3, b2[1, 3])
+    forward(1, C3, b2[1, C3])
     r[1] = backward(1)
-    r[0] = reduce_b(0, r[0])
     softmax_local(1)
     s = stats_start(1)
+    r[0] = reduce_b(0, r[0])
+    r[2] = backward(2)
     r[1] = reduce_b(1, r[1])
+    s = stats_next(1, s)
     r[0] = reduce_a(0, r[0])
-    r[2] = backward(2)
-    s = stats_next(1, 1, s)
+    r[3] = backward(3)
+    r[2] = reduce_b(2, r[2])
     r[1] = reduce_a(1, r[1])
-    reduce_x(0, r[0])
-    r[2] = reduce_b(2, r[2])
-    r[3] = backward(3)
-    s = stats_next(1, 2, s)
-    reduce_x(1, r[1])
-    r[3] = reduce_b(3, r[3])
-    r[2] = reduce_a(2, r[2])
     stats_end(1, s)
     gradient_logits(1)
     r[4] = backward(4)
-    r[3] = reduce_a(3, r[3])
-    reduce_x(2, r[2])
+    r[3] = reduce_b(3, r[3])
+    reduce_x(0, r[0])
+    r[2] = reduce_a(2, r[2])
     r[5] = backward(5)
     r[4] = reduce_b(4, r[4])
-    reduce_x(3, r[3])
+    reduce_x(1, r[1])
+    r[3] = reduce_a(3, r[3])
     r[6] = backward(6)
     r[5] = reduce_b(5, r[5])
+    reduce_x(2, r[2])
     r[4] = reduce_a(4, r[4])
     r[7] = backward(7)
     r[6] = reduce_b(6, r[6])
+    reduce_x(3, r[3])
     r[5] = reduce_a(5, r[5])
-    reduce_x(4, r[4])
     stores = fragment()
     loss()
     r[7] = reduce_b(7, r[7])
     r[6] = reduce_a(6, r[6])
+    reduce_x(4, r[4])
     reduce_x(5, r[5])
     r[7] = reduce_a(7, r[7])
     reduce_x(6, r[6])
@@ -402,22 +407,28 @@
         copy.wait()
 
 
+def hand_over(loss_in, grad_in, global_in, momentum_in, loss_out, grad_out, global_out, momentum_out):
+    loss_out[0] = loss_in[0]
+    grad_out[...] = grad_in[...]
+    global_out[...] = global_in[...]
+    momentum_out[...] = momentum_in[...]
+
+
 def body(hidden, targets, head, global_frag, momentum, peer_delta):
     own, depth = hidden.shape
     width = head.shape[1]
-    digits = jnp.stack([targets // 256, targets % 256], axis=1).astype(BF16)
-    ext = jnp.pad(digits, ((0, 0), (0, EXT - 2)))
     dma = pltpu.SemaphoreType.DMA
     pieces = 8
-    loss, grad, new_global, new_momentum = pl.pallas_call(
+    out_shape = (
+        jax.ShapeDtypeStruct((1,), F32),
+        jax.ShapeDtypeStruct((own, depth), BF16),
+        jax.ShapeDtypeStruct((FRAG, width), F32),
+        jax.ShapeDtypeStruct((FRAG, width), F32),
+    )
+    results = pl.pallas_call(
         kernel,
-        out_shape=(
-            jax.ShapeDtypeStruct((1,), F32),
-            jax.ShapeDtypeStruct((own, depth), BF16),
-            jax.ShapeDtypeStruct((FRAG, width), F32),
-            jax.ShapeDtypeStruct((FRAG, width), F32),
-        ),
-        in_specs=[pl.BlockSpec(memory_space=pl.ANY)] * 6,
+        out_shape=out_shape,
+        in_specs=[pl.BlockSpec(memory_space=pltpu.SMEM)] + [pl.BlockSpec(memory_space=pl.ANY)] * 5,
         out_specs=(
             pl.BlockSpec(memory_space=pltpu.SMEM),
             pl.BlockSpec(memory_space=pltpu.VMEM),
@@ -438,9 +449,8 @@
             pltpu.VMEM((pieces, 3, OWN, CHUNK), F32),
             pltpu.VMEM((pieces, OWN, CHUNK), F32),
             pltpu.VMEM((4, OWN, CHUNK), F32),
-            pltpu.VMEM((NX, NY, 8, 128), F32),
+            pltpu.VMEM((NX, NX, NY, 8, 128), F32),
             pltpu.VMEM((NX, NZ, 8, 128), F32),
-            pltpu.VMEM((NX, NX, 8, 128), F32),
             pltpu.VMEM((NX, 8, 128), F32),
             pltpu.VMEM((NX, HALF, 128), F32),
             pltpu.VMEM((HALF, 128), F32),
@@ -448,16 +458,16 @@
             pltpu.VMEM((FRAG, width), F32),
             pltpu.VMEM((FRAG, width), F32),
             pltpu.VMEM((FRAG, width), F32),
-            dma((2,)),
+            dma(()),
             dma((4,)),
             dma((3,)),
             dma((2,)),
-            dma((2,)),
-            dma((2, 2, 3, 2)),
+            dma((4, 2)),
+            dma((2, 4, 3, 2)),
+            dma((2, 4, 2, 2, 2)),
             dma((2, 4, 2, 2)),
-            dma((2, 4, 2, 2)),
-            dma((2, 7, 2)),
-            dma((pieces, 2, 2)),
+            dma((2, 10, 2)),
+            dma((pieces, 2, 2, 2)),
             dma((pieces, 2, 2)),
             dma((pieces, 3, 2)),
             dma((4, 2)),
@@ -466,8 +476,14 @@
             collective_id=0, has_side_effects=True, vmem_limit_bytes=62 << 20
         ),
         cost_estimate=pl.CostEstimate(flops=18 * 10**9, bytes_accessed=24 * 2**20, transcendentals=2**20),
-    )(hidden, ext, head, global_frag, momentum, peer_delta)
-    return loss, grad, new_global, new_momentum
+    )(targets, hidden, head, global_frag, momentum, peer_delta)
+    scalar = pl.BlockSpec(memory_space=pltpu.SMEM)
+    grad_block = pl.BlockSpec((own, depth // PARTS), lambda i: (0, i))
+    frag_block = pl.BlockSpec((FRAG // PARTS, width), lambda i: (i, 0))
+    specs = (scalar, grad_block, frag_block, frag_block)
+    return pl.pallas_call(
+        hand_over, out_shape=out_shape, grid=(PARTS,), in_specs=specs, out_specs=specs
+    )(*results)
 
 
 def solution(mesh):

time: 123 us -> 103 us (0.84)
  Pallas kernels: 112 us -> 102 us
  local copies, waits for them, and re-layouts: 6.86 us -> 0 us
  between operations: 2.39 us -> 0.64 us
    pallas_call x1 -> x2, Pallas kernels: 112 us -> 102 us  [the longest x1 97.2 us: body(): pl.pallas_call(kernel, out_shape=out_shape, in_specs=[pl.BlockSpec(memory...]
    unnamed x3 -> x0, local copies, waits for them, and re-layouts: 6.16 us -> none
where the time goes in v2:
time: 103 us; the launch traced here: 102 us
  Pallas kernels  102 us (99%)
    pallas_call x1, Pallas kernels, body(): pl.pallas_call(kernel, out_shape=out_shape, in_specs=[pl.BlockSpec(memory...  97.2 us
    pallas_call x1, Pallas kernels, body(): pl.pallas_call(hand_over, out_shape=out_shape, grid=(PARTS,), in_specs=sp...  4.45 us

profile of v2, /device:TPU:6, one launch (start us, length us, event | category | flops | bytes accessed | tf_op | source)
XLA Modules:
  0.0 102.3 jit_solution(14851615741828005039)
XLA Ops:
  0.6 97.2 %shard_map.93 = (f32[1]{0:T(128)}, bf16[16,4096]{1,0:T(8,128)(2,1)}, f32[128,2048]{1,0:T(8,128)}, f32[128,2048]{1,0:T(8,128)}) custom-call(s32[16]{0:T(128)} %targets_ref.1, bf16[16,4096]{1,0:T(8,128)(2,1)} %hidden_hbm.1, bf16[4096,2048]{1,0:T(8,128)(2,1)} %head_hbm.1, f32[128,2048]{1,0:T(8,128)} %global_hbm.1, f32[128,2048]{1,0:T(8,128)} %momentum_hbm.1, ...), custom_call_target="tpu_custom_call" | custom-call | flops 17999998976 | bytes 25165824 | tf_op jit(solution)/shard_map/pallas_call | solution.py:428
  97.9 4.5 %shard_map.94 = (f32[1]{0:T(128)}, bf16[16,4096]{1,0:T(8,128)(2,1)}, f32[128,2048]{1,0:T(8,128)}, f32[128,2048]{1,0:T(8,128)}) custom-call(f32[1]{0:T(128)} %get-tuple-element.8.loss_in, bf16[16,4096]{1,0:T(8,128)(2,1)} %get-tuple-element.9.grad_in, f32[128,2048]{1,0:T(8,128)} %get-tuple-element.10.global_in, f32[128,2048]{1,0:T(8,128)} %get-tuple-element.11.momentum_in), custom_call_target="tpu_custom_call" | custom-call | tf_op jit(solution)/shard_map/pallas_call | solution.py:484

commit v3 on v2

--- a/solution.py
+++ b/solution.py
@@ -66,6 +66,12 @@
     def arrived(copies):
         for copy in copies:
             copy.wait_recv()
+
+    barrier = pltpu.get_barrier_semaphore()
+    plane = [(dx, dy) for dx in range(NX) for dy in range(NY) if dx or dy]
+    partners = [dev(dz=d) for d in (1, 2, 3)] + [dev(dx=dx, dy=dy) for dx, dy in plane]
+    for partner in partners:
+        pl.semaphore_signal(barrier, inc=1, device_id=partner, device_id_type=MESH)
 
     load = pltpu.make_async_copy(hidden_hbm, g_buf.at[xh, y, z, :, pl.ds(0, 4 * CHUNK)], load_sem)
     load.start()
@@ -80,12 +86,6 @@
     ]
     for copy in frag_loads:
         copy.start()
-
-    barrier = pltpu.get_barrier_semaphore()
-    plane = [(dx, dy) for dx in range(NX) for dy in range(NY) if dx or dy]
-    partners = [dev(dz=d) for d in (1, 2, 3)] + [dev(dx=dx, dy=dy) for dx, dy in plane]
-    for partner in partners:
-        pl.semaphore_signal(barrier, inc=1, device_id=partner, device_id_type=MESH)
 
     row = lax.broadcasted_iota(jnp.int32, (OWN, EXT), 0)
     lane = lax.broadcasted_iota(jnp.int32, (OWN, EXT), 1)
@@ -351,53 +351,54 @@
     for c in (C0, C1): b2[1, c] = gather_b2(1, c, b1[1, c])
     forward(0, C2, b2[0, C2])
     forward(0, C3, b2[0, C3])
+    for c in (C2, C3): b2[1, c] = gather_b2(1, c, b1[1, c])
     softmax_local(0)
-    s = stats_start(0)
-    for c in (C2, C3): b2[1, c] = gather_b2(1, c, b1[1, c])
+    s0 = stats_start(0)
     forward(1, C0, b2[1, C0])
     forward(1, C1, b2[1, C1])
-    s = stats_next(0, s)
+    s0 = stats_next(0, s0)
     forward(1, C2, b2[1, C2])
-    stats_end(0, s)
+    forward(1, C3, b2[1, C3])
+    softmax_local(1)
+    s1 = stats_start(1)
+    stats_end(0, s0)
     gradient_logits(0)
-    r = {0: backward(0)}
-    forward(1, C3, b2[1, C3])
+    r = {}
+    r[0] = backward(0)
     r[1] = backward(1)
-    softmax_local(1)
-    s = stats_start(1)
+    r[2] = backward(2)
+    r[3] = backward(3)
+    s1 = stats_next(1, s1)
     r[0] = reduce_b(0, r[0])
-    r[2] = backward(2)
     r[1] = reduce_b(1, r[1])
-    s = stats_next(1, s)
-    r[0] = reduce_a(0, r[0])
-    r[3] = backward(3)
     r[2] = reduce_b(2, r[2])
-    r[1] = reduce_a(1, r[1])
-    stats_end(1, s)
+    r[3] = reduce_b(3, r[3])
+    stats_end(1, s1)
     gradient_logits(1)
     r[4] = backward(4)
-    r[3] = reduce_b(3, r[3])
+    r[0] = reduce_a(0, r[0])
+    r[5] = backward(5)
+    r[1] = reduce_a(1, r[1])
+    r[6] = backward(6)
+    r[2] = reduce_a(2, r[2])
+    r[7] = backward(7)
+    r[3] = reduce_a(3, r[3])
+    r[4] = reduce_b(4, r[4])
     reduce_x(0, r[0])
-    r[2] = reduce_a(2, r[2])
-    r[5] = backward(5)
-    r[4] = reduce_b(4, r[4])
+    r[5] = reduce_b(5, r[5])
     reduce_x(1, r[1])
-    r[3] = reduce_a(3, r[3])
-    r[6] = backward(6)
-    r[5] = reduce_b(5, r[5])
+    r[6] = reduce_b(6, r[6])
     reduce_x(2, r[2])
+    r[7] = reduce_b(7, r[7])
+    reduce_x(3, r[3])
     r[4] = reduce_a(4, r[4])
-    r[7] = backward(7)
-    r[6] = reduce_b(6, r[6])
-    reduce_x(3, r[3])
     r[5] = reduce_a(5, r[5])
+    r[6] = reduce_a(6, r[6])
+    r[7] = reduce_a(7, r[7])
     stores = fragment()
     loss()
-    r[7] = reduce_b(7, r[7])
-    r[6] = reduce_a(6, r[6])
     reduce_x(4, r[4])
     reduce_x(5, r[5])
-    r[7] = reduce_a(7, r[7])
     reduce_x(6, r[6])
     reduce_x(7, r[7])
     finish()
@@ -407,11 +408,23 @@
         copy.wait()
 
 
-def hand_over(loss_in, grad_in, global_in, momentum_in, loss_out, grad_out, global_out, momentum_out):
+def hand_over(loss_in, grad_in, global_in, momentum_in, loss_out, grad_out, global_out, momentum_out, grad, frag, sem):
+    moves = [(grad_in, grad, grad_out)]
+    step = FRAG // PARTS
+    for i in range(PARTS):
+        rows = pl.ds(i * step, step)
+        for j, (src, dst) in enumerate(((global_in, global_out), (momentum_in, momentum_out))):
+            moves.append((src.at[rows], frag.at[j, rows], dst.at[rows]))
+    reads = [pltpu.make_async_copy(src, held, sem.at[0, i]) for i, (src, held, _) in enumerate(moves)]
+    writes = [pltpu.make_async_copy(held, dst, sem.at[1, i]) for i, (_, held, dst) in enumerate(moves)]
+    for read in reads:
+        read.start()
     loss_out[0] = loss_in[0]
-    grad_out[...] = grad_in[...]
-    global_out[...] = global_in[...]
-    momentum_out[...] = momentum_in[...]
+    for read, write in zip(reads, writes):
+        read.wait()
+        write.start()
+    for write in writes:
+        write.wait()
 
 
 def body(hidden, targets, head, global_frag, momentum, peer_delta):
@@ -477,12 +490,17 @@
         ),
         cost_estimate=pl.CostEstimate(flops=18 * 10**9, bytes_accessed=24 * 2**20, transcendentals=2**20),
     )(targets, hidden, head, global_frag, momentum, peer_delta)
-    scalar = pl.BlockSpec(memory_space=pltpu.SMEM)
-    grad_block = pl.BlockSpec((own, depth // PARTS), lambda i: (0, i))
-    frag_block = pl.BlockSpec((FRAG // PARTS, width), lambda i: (i, 0))
-    specs = (scalar, grad_block, frag_block, frag_block)
+    specs = (pl.BlockSpec(memory_space=pltpu.SMEM),) + (pl.BlockSpec(memory_space=pl.ANY),) * 3
     return pl.pallas_call(
-        hand_over, out_shape=out_shape, grid=(PARTS,), in_specs=specs, out_specs=specs
+        hand_over,
+        out_shape=out_shape,
+        in_specs=specs,
+        out_specs=specs,
+        scratch_shapes=[
+            pltpu.VMEM((own, depth), BF16),
+            pltpu.VMEM((2, FRAG, width), F32),
+            dma((2, 1 + 2 * PARTS)),
+        ],
     )(*results)
 
 

time: 103 us -> 95 us (0.922)
  Pallas kernels: 102 us -> 94.1 us
    pallas_call x1, Pallas kernels: 97.2 us -> 90.4 us  [body(): pl.pallas_call(kernel, out_shape=out_shape, in_specs=[pl.BlockSpec(memory...]
where the time goes in v3:
time: 95 us; the launch traced here: 94.9 us
  Pallas kernels  94.1 us (99%)
    pallas_call x1, Pallas kernels, body(): pl.pallas_call(kernel, out_shape=out_shape, in_specs=[pl.BlockSpec(memory...  90.4 us
    pallas_call x1, Pallas kernels, body(): pl.pallas_call(hand_over, out_shape=out_shape, in_specs=specs, out_specs=...  3.63 us

profile of v3, /device:TPU:6, one launch (start us, length us, event | category | flops | bytes accessed | tf_op | source)
XLA Modules:
  0.0 94.9 jit_solution(10701503392320109577)
XLA Ops:
  0.6 90.4 %shard_map.93 = (f32[1]{0:T(128)}, bf16[16,4096]{1,0:T(8,128)(2,1)}, f32[128,2048]{1,0:T(8,128)}, f32[128,2048]{1,0:T(8,128)}) custom-call(s32[16]{0:T(128)} %targets_ref.1, bf16[16,4096]{1,0:T(8,128)(2,1)} %hidden_hbm.1, bf16[4096,2048]{1,0:T(8,128)(2,1)} %head_hbm.1, f32[128,2048]{1,0:T(8,128)} %global_hbm.1, f32[128,2048]{1,0:T(8,128)} %momentum_hbm.1, ...), custom_call_target="tpu_custom_call" | custom-call | flops 17999998976 | bytes 25165824 | tf_op jit(solution)/shard_map/pallas_call | solution.py:441
  91.1 3.6 %shard_map.94 = (f32[1]{0:T(128)}, bf16[16,4096]{1,0:T(8,128)(2,1)}, f32[128,2048]{1,0:T(8,128)}, f32[128,2048]{1,0:T(8,128)}) custom-call(f32[1]{0:T(128)} %get-tuple-element.8.loss_in, bf16[16,4096]{1,0:T(8,128)(2,1)} %get-tuple-element.9.grad_in, f32[128,2048]{1,0:T(8,128)} %get-tuple-element.10.global_in, f32[128,2048]{1,0:T(8,128)} %get-tuple-element.11.momentum_in), custom_call_target="tpu_custom_call" | custom-call | tf_op jit(solution)/shard_map/pallas_call | solution.py:494

commit v4 on v3

--- a/solution.py
+++ b/solution.py
@@ -18,7 +18,7 @@
 CHUNK = 1024
 EXT = 128
 TILE = 512
-PARTS = 4
+PARTS = 1
 ORDER = (0, 2, 1, 3)
 
 
@@ -155,7 +155,7 @@
         return (t[:, 0:1] * 256.0 + t[:, 1:2]).astype(jnp.int32) - base
 
     def softmax_local(h):
-        @pl.loop(0, HALF // STEP)
+        @pl.loop(0, HALF // STEP, unroll=2)
         def _(i):
             rows = pl.ds(pl.multiple_of(i * STEP, STEP), STEP)
             values = logits[h, rows, :]
@@ -211,7 +211,7 @@
             scale = jnp.exp(col_top[h, 128 * i : 128 * (i + 1), :] - top) / (total * row_count)
             col_sum[128 * i : 128 * (i + 1), :] = scale
 
-        @pl.loop(0, HALF // STEP)
+        @pl.loop(0, HALF // STEP, unroll=2)
         def _(i):
             rows = pl.ds(pl.multiple_of(i * STEP, STEP), STEP)
             target = target_columns(h, i)

time: 95 us -> 93.5 us (0.984)
  Pallas kernels: 94.1 us -> 92.5 us
    pallas_call x1, Pallas kernels: 90.4 us -> 88.7 us  [body(): pl.pallas_call(kernel, out_shape=out_shape, in_specs=[pl.BlockSpec(memory...]
where the time goes in v4:
time: 93.5 us; the launch traced here: 93.3 us
  Pallas kernels  92.5 us (99%)
    pallas_call x1, Pallas kernels, body(): pl.pallas_call(kernel, out_shape=out_shape, in_specs=[pl.BlockSpec(memory...  88.7 us
    pallas_call x1, Pallas kernels, body(): pl.pallas_call(hand_over, out_shape=out_shape, in_specs=specs, out_specs=...  3.82 us

profile of v4, /device:TPU:6, one launch (start us, length us, event | category | flops | bytes accessed | tf_op | source)
XLA Modules:
  0.0 93.3 jit_solution(1388905812940012025)
XLA Ops:
  0.6 88.7 %shard_map.93 = (f32[1]{0:T(128)}, bf16[16,4096]{1,0:T(8,128)(2,1)}, f32[128,2048]{1,0:T(8,128)}, f32[128,2048]{1,0:T(8,128)}) custom-call(s32[16]{0:T(128)} %targets_ref.1, bf16[16,4096]{1,0:T(8,128)(2,1)} %hidden_hbm.1, bf16[4096,2048]{1,0:T(8,128)(2,1)} %head_hbm.1, f32[128,2048]{1,0:T(8,128)} %global_hbm.1, f32[128,2048]{1,0:T(8,128)} %momentum_hbm.1, ...), custom_call_target="tpu_custom_call" | custom-call | flops 17999998976 | bytes 25165824 | tf_op jit(solution)/shard_map/pallas_call | solution.py:441
  89.3 3.8 %shard_map.94 = (f32[1]{0:T(128)}, bf16[16,4096]{1,0:T(8,128)(2,1)}, f32[128,2048]{1,0:T(8,128)}, f32[128,2048]{1,0:T(8,128)}) custom-call(f32[1]{0:T(128)} %get-tuple-element.8.loss_in, bf16[16,4096]{1,0:T(8,128)(2,1)} %get-tuple-element.9.grad_in, f32[128,2048]{1,0:T(8,128)} %get-tuple-element.10.global_in, f32[128,2048]{1,0:T(8,128)} %get-tuple-element.11.momentum_in), custom_call_target="tpu_custom_call" | custom-call | tf_op jit(solution)/shard_map/pallas_call | solution.py:494
